TPU v7x, 512 devices: a whole 4x4x16 slice. The times are simulated.
512 devices in a mesh: row: 32 (over z_hi, x, y), tp: 16 (over z_lo, core).
Axes of the slice: x: 4, y: 4, z: 16 (z_hi: 2, z_lo: 8; z = z_hi * 8 + z_lo), core: 2. Of those that a mesh axis runs over, the one named last changes fastest.
Arguments:
- tokens: bfloat16 [8192, 4096], P('row', 'tp'), may hold values from -6 to 6
- w_query: bfloat16 [4096, 4096], P(None, 'tp'), may hold values from -0.09375 to 0.09375
- w_keyval: bfloat16 [4096, 4096], P(None, 'tp'), may hold values from -1 to 1, as said below
- prefix_cache: bfloat16 [32, 1024, 4096], P('row', None, 'tp'), may hold values from -1000 to 1000, as said below
- prefix_len: int32 [32], P('row'), may hold values from 2 to 1024, as said below
- page_owner: int32 [512, 2], P('row'), may hold values from 0 to 31, all different within a row; in each aligned block of 16 rows (0 to 15, 16 to 31, ...) at most 2 rows name the same one
Outputs:
- context: bfloat16 [8192, 4096], P('row', 'tp')
- page_store: bfloat16 [2048, 16, 2048], P('row', None, 'tp')
Inputs may be any that keep to these rules, and one draw needn't show every extreme that they name: `prefix_len`: no row is given more than 1024 cached positions, and some row exactly 1024. `prefix_cache`: the 2 stored copies of each key head are equal. `w_keyval`: the 2 stored copies of each key head's columns are equal. `page_owner`: the two owners of a page differ. Among the 16 pages of one row no owner is named more than 2 times, and in some row one owner exactly 2 times.
All inputs are finite; a program needn't handle non-finite values.
Results may differ from a plain program's by a relative error of at most 0.025.
Values may be sent and summed in bfloat16 or wider, within the bound.
No kernel may reach another device: no remote copies, remote signals or barrier semaphores. Data moves between devices by JAX's collectives and lax.ppermute only.
A program may use at most 64 MiB of HBM per device.

v0:
```python
import jax
import jax.numpy as jnp
from jax import lax
from jax.sharding import PartitionSpec as P

HD = 128
PAGE = 16
KBLK = 512


ROPE_BASE = 500000.0


def rotate(values, positions):
    half = values.shape[-1] // 2
    inverse = ROPE_BASE ** (-(jnp.arange(half, dtype=jnp.float32) * 2.0 / values.shape[-1]))
    angles = positions[..., None] * inverse
    cosine = jnp.cos(angles)[..., None, :]
    sine = jnp.sin(angles)[..., None, :]
    first = values[..., :half]
    second = values[..., half:]
    return jnp.concatenate(
        [first * cosine - second * sine, second * cosine + first * sine], axis=-1
    )


def shards(tokens, w_query, w_keyval, prefix_cache, prefix_len, page_owner):
    token_count = tokens.shape[0]
    query_cols = w_query.shape[1]
    kv_cols = w_keyval.shape[1]
    piece = lax.all_gather(tokens, "tp", axis=1, tiled=True)
    query = jnp.dot(piece, w_query, preferred_element_type=jnp.float32)
    keyval = jnp.dot(piece, w_keyval, preferred_element_type=jnp.float32)
    length = prefix_len[0]
    positions = length.astype(jnp.float32) + jnp.arange(token_count, dtype=jnp.float32)
    heads_local = query_cols // HD
    kv_local = kv_cols // (2 * HD)
    paired = keyval.reshape(token_count, kv_local, 2, HD)
    new_keys = rotate(paired[:, :, 0], positions).astype(jnp.bfloat16)
    new_values = paired[:, :, 1].astype(jnp.bfloat16)
    prefix_rows = prefix_cache.shape[1]
    old_pairs = prefix_cache[0].reshape(prefix_rows, kv_local, 2, HD)
    old_keys = old_pairs[:, :, 0]
    old_values = old_pairs[:, :, 1]
    groups = heads_local // kv_local
    queries = (
        rotate(query.reshape(token_count, heads_local, HD), positions) * HD ** (-0.5)
    ).astype(jnp.bfloat16)
    queries = jnp.transpose(queries.reshape(token_count, kv_local, groups, HD), (1, 0, 2, 3))
    queries = queries.reshape(kv_local, token_count * groups, HD)
    query_token = jnp.arange(token_count * groups, dtype=jnp.int32) // groups
    fresh_scores = jnp.einsum("kqd,skd->kqs", queries, new_keys, preferred_element_type=jnp.float32)
    causal = (jnp.arange(token_count, dtype=jnp.int32)[None, :] <= query_token[:, None])[None, :, :]
    highest = jnp.max(jnp.where(causal, fresh_scores, -jnp.inf), axis=-1)
    block_count = prefix_rows // KBLK

    def max_step(block, carried):
        running, kept = carried
        offset = block * KBLK
        keys_block = lax.dynamic_slice_in_dim(old_keys, offset, KBLK, 0)
        scores = jnp.einsum("kqd,skd->kqs", queries, keys_block, preferred_element_type=jnp.float32)
        valid = (offset + jnp.arange(KBLK, dtype=jnp.int32) < length)[None, None, :]
        masked = jnp.where(valid, scores, -jnp.inf)
        kept = lax.dynamic_update_index_in_dim(kept, masked, block, 0)
        return (jnp.maximum(running, jnp.max(masked, axis=-1)), kept)

    kept_scores = jnp.full(
        (block_count, kv_local, token_count * groups, KBLK), -jnp.inf, jnp.float32
    )
    highest, kept_scores = lax.fori_loop(0, block_count, max_step, (highest, kept_scores))
    fresh_weights = jnp.where(causal, jnp.exp(fresh_scores - highest[..., None]), 0.0)
    total = jnp.sum(fresh_weights, axis=-1)
    mixed = jnp.einsum(
        "kqs,skd->kqd",
        fresh_weights.astype(jnp.bfloat16),
        new_values,
        preferred_element_type=jnp.float32,
    )

    def sum_step(block, carried):
        running_total, running_mixed = carried
        masked = lax.dynamic_index_in_dim(kept_scores, block, 0, keepdims=False)
        weights = jnp.exp(masked - highest[..., None])
        values_block = lax.dynamic_slice_in_dim(old_values, block * KBLK, KBLK, 0)
        product = jnp.einsum(
            "kqs,skd->kqd",
            weights.astype(jnp.bfloat16),
            values_block,
            preferred_element_type=jnp.float32,
        )
        return (running_total + jnp.sum(weights, axis=-1), running_mixed + product)

    total, mixed = lax.fori_loop(0, block_count, sum_step, (total, mixed))
    context = (mixed / total[..., None]).reshape(kv_local, token_count, groups, HD)
    context = (
        jnp.transpose(context, (1, 0, 2, 3)).reshape(token_count, query_cols).astype(jnp.bfloat16)
    )
    own = jnp.stack([new_keys, new_values], axis=2)
    key_side = lax.axis_index("tp") % 2 == 0
    own_store = jnp.where(key_side, own[:, 0, 0], own[:, 0, 1])
    store_cols = own_store.shape[-1]
    page_rows = page_owner.shape[0]
    row_count = lax.axis_size("row")
    most = max(2, 4 * page_rows // row_count)
    page_data = own_store.reshape(page_rows, PAGE * store_cols)
    flat_owner = page_owner.reshape(-1)
    onehot = (flat_owner[:, None] == jnp.arange(row_count, dtype=jnp.int32)[None, :]).astype(
        jnp.int32
    )
    rank = jnp.sum((jnp.cumsum(onehot, axis=0) - onehot) * onehot, axis=1)
    slot = flat_owner * most + rank
    placed = jnp.arange(row_count * most, dtype=jnp.int32)[:, None] == slot[None, :]
    copies = jnp.repeat(page_data, 2, axis=0)
    packed = jnp.dot(placed.astype(jnp.bfloat16), copies, preferred_element_type=jnp.float32)
    received = lax.all_to_all(
        packed.astype(jnp.bfloat16).reshape(row_count, most * PAGE * store_cols),
        "row",
        split_axis=0,
        concat_axis=0,
        tiled=True,
    )
    return (context, received.reshape(row_count * most, PAGE, store_cols))


def solution(mesh):
    return jax.shard_map(
        shards,
        mesh=mesh,
        in_specs=(
            P("row", "tp"),
            P(None, "tp"),
            P(None, "tp"),
            P("row", None, "tp"),
            P("row"),
            P("row", None),
        ),
        out_specs=(P("row", "tp"), P("row", None, "tp")),
        check_vma=False,
    )
```

profile of v0, /device:TPU:2, one launch (start us, length us, event | category | flops | bytes accessed | tf_op | source)
XLA Modules:
  0.0 157.3 jit_solution(3770380989080072376)
XLA Ops:
  7.2 0.7 all-gather.2.cloned.1.call-update
  8.6 0.8 copy.40
  9.6 1.3 copy.35
  10.9 0.8 copy.38
  11.7 0.2 select_reduce_fusion.1
  11.9 0.5 multiply_cosine_fusion.1
  12.5 86.1 %all-gather.2.cloned.1.call-done = bf16[256,4096]{1,0:T(8,128)(2,1)} async-done(((bf16[256,256]{1,0:T(8,128)(2,1)}), bf16[256,4096]{1,0:T(8,128)(2,1)}) %all-gather.2.cloned.1.call-update) | async-done | bytes 2097168 | tf_op jit(solution)/shard_map/all_gather | solution.py:31
  98.6 2.7 %fusion.45 = f32[256,256]{0,1:T(8,128)S(1)} fusion(bf16[256,4096]{1,0:T(8,128)(2,1)} %all-gather.2.cloned.1.call-done, bf16[4096,256]{1,0:T(8,128)(2,1)S(1)} %copy-done), kind=kOutput, calls=%fused_computation.76 | convolution fusion | flops 536870912 | bytes 4456448 | tf_op jit(solution)/shard_map/dot_general | solution.py:33
  101.3 0.1 copy-done.2
  101.5 1.0 fusion.44
  102.5 0.1 copy.47
  102.7 0.6 fusion.26
  103.3 0.1 maximum_convert_fusion
  103.4 0.1 copy.45
  103.6 0.1 copy.44
  103.8 0.3 multiply_subtract_fusion
  104.0 0.1 fusion.17
  104.2 0.4 select_reduce_fusion
  104.5 4.2 %while.30 = (s32[]{:T(128)}, f32[1,512]{1,0:T(1,128)S(1)}, f32[2,1,512,512]{2,3,1,0:T(8,128)}, s32[]{:T(128)}, bf16[1024,1,128]{0,2,1:T(8,128)(2,1)S(1)}, /*inde...) while((s32[]{:T(128)}, f32[1,512]{1,0:T(1,128)S(1)}, ...), condition=%wide.region_3.4_spmd, body=%wide.region_1.3_spmd.sunk | while | flops 67634184 | bytes 3417259 | solution.py:70
  104.6 0.7 add_compare_fusion.2
  105.2 0.4 fusion.57
  105.6 1.1 bitcast_dynamic-update-slice_fusion.2
  106.7 0.7 add_compare_fusion.2
  107.3 0.4 fusion.57
  107.7 1.1 bitcast_dynamic-update-slice_fusion.2
  108.8 0.1 fusion.14
  108.9 0.3 convolution_bitcast_fusion.1
  109.4 0.2 convolution_convert_fusion
  109.6 0.5 all_to_all.8
  110.1 0.5 broadcast.194
  110.6 2.1 %reduce.13 = bf16[32,4096]{1,0:T(8,128)(2,1)S(1)} reduce(bf16[32,1,4096]{2,1,0:T(2,128)(2,1)S(1)} %all_to_all.8, bf16[]{:T(256)} %broadcast.194), dimensions={1}, to_apply=%all_to_all.8.reduce_sub_computation | reduce | bytes 524290 | tf_op jit(solution)/shard_map/all_to_all | solution.py:115
  112.7 0.9 reshape.338
  113.6 15.7 %all-to-all-start = ((bf16[32,2,2048]{2,1,0:T(2,128)(2,1)}), bf16[32,2,2048]{2,1,0:T(2,128)(2,1)}, u32[]{:S(2)}, u32[]{:S(2)}) async-start(bf16[32,2,2048]{2,1,0:T(2,128)(2,1)} %reshape.338), calls=%async_computation | async-start | bytes 524288 | tf_op jit(solution)/shard_map/all_to_all | solution.py:115
  129.3 10.9 %while.31 = (s32[]{:T(128)}, f32[1,512]{1,0:T(1,128)S(1)}, f32[1,512,128]{2,1,0:T(8,128)S(1)}, f32[2,1,512,512]{2,3,1,0:T(8,128)}, f32[1,512]{1,0:T(1,128)S(1)},...) while((s32[]{:T(128)}, f32[1,512]{1,0:T(1,128)S(1)}, ...), condition=%wide.region_7.8_spmd, body=%wide.region_5.7_spmd.sunk | while | flops 68222984 | bytes 6959267 | solution.py:93
  129.3 2.3 %constant_dynamic-slice_fusion.2 = f32[1,1,512,512]{2,3,1,0:T(8,128)} fusion(f32[2,1,512,512]{2,3,1,0:T(8,128)} %get-tuple-element.443, s32[]{:T(128)S(6)} %copy.63), kind=kLoop, calls=%fused_computation.18.clone.1 | loop fusion | bytes 2097156 | tf_op jit(solution)/shard_map/while/body/eval_jaxpr/jit(dynamic_index_in_dim)/dynamic_slice | solution.py:82
  131.6 1.6 copy.49
  133.1 0.3 fusion.60
  133.4 1.3 fusion.61
  134.8 2.3 %constant_dynamic-slice_fusion.2 = f32[1,1,512,512]{2,3,1,0:T(8,128)} fusion(f32[2,1,512,512]{2,3,1,0:T(8,128)} %get-tuple-element.443, s32[]{:T(128)S(6)} %copy.63), kind=kLoop, calls=%fused_computation.18.clone.1 | loop fusion | bytes 2097156 | tf_op jit(solution)/shard_map/while/body/eval_jaxpr/jit(dynamic_index_in_dim)/dynamic_slice | solution.py:82
  137.0 1.6 copy.49
  138.6 0.3 fusion.60
  138.9 1.3 fusion.61
  140.2 0.1 divide_convert_fusion
  140.4 0.7 convert_element_type.79
  141.1 4.8 %all-to-all-done = bf16[32,2,2048]{2,1,0:T(2,128)(2,1)} async-done(((bf16[32,2,2048]{2,1,0:T(2,128)(2,1)}), bf16[32,2,2048]{2,1,0:T(2,128)(2,1)}, u32[]{:S(2)}, u32[]{:S(2)}) %all-to-all-start) | async-done | bytes 262176 | tf_op jit(solution)/shard_map/all_to_all | solution.py:115
  145.9 2.2 %reshape.339 = bf16[32,1,4096]{2,1,0:T(2,128)(2,1)S(1)} reshape(bf16[32,2,2048]{2,1,0:T(2,128)(2,1)} %all-to-all-done) | data formatting | bytes 524288
  148.1 1.5 reduce.12
  149.6 0.8 reshape.336
  (28 shorter events, 0.7 us)
Async XLA Ops:
  7.2 91.5 %copy-start = (bf16[4096,256]{1,0:T(8,128)(2,1)S(1)}, bf16[4096,256]{1,0:T(8,128)(2,1)}, u32[]{:S(2)}) copy-start(bf16[4096,256]{1,0:T(8,128)(2,1)} %param.12) | copy-start | bytes 6291460
  7.2 91.4 %all-gather.2.cloned.1.call-start = ((), (), s32[]{:S(2)}) async-start(), calls=%async_computation.1 | async-start | bytes 2228224 | tf_op jit(solution)/shard_map/all_gather | solution.py:31
  98.6 2.7 %copy-start.1 = (bf16[256,4096]{1,0:T(8,128)(2,1)S(1)}, bf16[256,4096]{1,0:T(8,128)(2,1)}, u32[]{:S(2)}) copy-start(bf16[256,4096]{1,0:T(8,128)(2,1)} %all-gather.2.cloned.1.call-done) | copy-start | bytes 6291460
  98.6 2.9 %copy-start.2 = (bf16[4096,256]{1,0:T(8,128)(2,1)S(1)}, bf16[4096,256]{1,0:T(8,128)(2,1)}, u32[]{:S(2)}) copy-start(bf16[4096,256]{1,0:T(8,128)(2,1)} %param.11) | copy-start | bytes 6291460
  113.6 32.3 %all-to-all-start = ((bf16[32,2,2048]{2,1,0:T(2,128)(2,1)}), bf16[32,2,2048]{2,1,0:T(2,128)(2,1)}, u32[]{:S(2)}, u32[]{:S(2)}) async-start(bf16[32,2,2048]{2,1,0:T(2,128)(2,1)} %reshape.338), calls=%async_computation | async-start | bytes 524288 | tf_op jit(solution)/shard_map/all_to_all | solution.py:115
Sparse Core Ops, SparseCore 0:
  10.0 88.5 all-gather.1
where the time goes:
time: 158 us; the launch traced here: 157 us
  waiting for transfers between devices  91.7 us (58%)
  local copies, waits for them, and re-layouts  19.2 us (12%)
  starting transfers between devices  15.7 us (10%)
  between operations  15 us (9%)
  other arithmetic  7.85 us (5%)
  matrix products  7.74 us (5%)
    all_gather x1, waiting for transfers between devices, shards(): piece = lax.all_gather(tokens, 'tp', axis=1, tiled=True)  86.1 us
    all_to_all x1, starting transfers between devices, shards(): lax.all_to_all(packed.astype(jnp.bfloat16).reshape(row_count, most * PAGE...  15.7 us
    dynamic_slice x4, local copies, waits for them, and re-layouts, sum_step(): masked = lax.dynamic_index_in_dim(kept_scores, block, 0, keepdims=False)  7.67 us
    unnamed x14, local copies, waits for them, and re-layouts  5.71 us
    all_to_all x1, waiting for transfers between devices, shards(): lax.all_to_all(packed.astype(jnp.bfloat16).reshape(row_count, most * PAGE...  4.85 us
    all_to_all x2, other arithmetic, shards(): lax.all_to_all(packed.astype(jnp.bfloat16).reshape(row_count, most * PAGE...  3.67 us
  transfers between devices with their start and end apart: 2, of which 2 were waited for; matrix products, arithmetic and copies ran while one was open for 10% of the time, Pallas kernels for 0%

commit v1 on v0

v1 whole, which is shorter than its diff:
```python
import functools
import jax
import jax.numpy as jnp
from jax import lax
from jax.experimental import pallas as pl
from jax.experimental.pallas import tpu as pltpu
from jax.sharding import PartitionSpec as P

HD = 128
PAGE = 16
ROPE_BASE = 500000.0
CHIPS = 8
ROWS = 256
BLOCK = 512
STEPS = ((3, 0), (1, 0), (2, 1), (4, 3), (6, 3), (5, 4), (7, 6))
EARLY = (1, 2, 3, 4)
LATE = (5, 6, 7)
BF = jnp.bfloat16
F32 = jnp.float32


def step_perm(got, held):
    hop = got - held
    right = [(2 * c, 2 * (c + hop)) for c in range(CHIPS) if c >= held and c + hop < CHIPS]
    left = [
        (2 * c + 1, 2 * (c - hop) + 1) for c in range(CHIPS) if c + held < CHIPS and c >= hop
    ]
    return right + left


def partial_kernel(count, first, rows_ref, *refs):
    blocks, refs = refs[:count], refs[count:]
    weights, refs = refs[:3], refs[3:]
    given, outs = refs[: len(refs) - 3], refs[len(refs) - 3 :]
    step = pl.program_id(0)

    def add(block):
        for j in range(3):
            product = jnp.dot(block[0:ROWS], weights[j][0:256], preferred_element_type=F32)
            product += jnp.dot(block[ROWS:], weights[j][256:], preferred_element_type=F32)
            outs[j][...] += product

    @pl.when(step == 0)
    def _():
        if first:
            own, given_weights = given[0], given[1:]
            for j in range(3):
                outs[j][...] = jnp.dot(
                    own[...], given_weights[j][...], preferred_element_type=F32
                )
        else:
            for j in range(3):
                outs[j][...] = given[j][...]

    for s in range(count):
        pl.when(step == s)(functools.partial(add, blocks[s]))


def partial_sums(rows, blocks, weights, given, first):
    count = len(blocks)
    whole = lambda s, r: (0, 0)
    in_specs = [pl.BlockSpec((2 * ROWS, 256), whole)] * count
    in_specs += [pl.BlockSpec((BLOCK, 256), lambda s, r: (r[s], 0))] * 3
    if first:
        in_specs += [pl.BlockSpec((ROWS, 256), whole)]
        in_specs += [pl.BlockSpec((256, 256), lambda s, r: (r[count], 0))] * 3
        given = [given] + list(weights)
    else:
        in_specs += [pl.BlockSpec((ROWS, 256), whole)] * 3
    return pl.pallas_call(
        functools.partial(partial_kernel, count, first),
        out_shape=[jax.ShapeDtypeStruct((ROWS, 256), F32)] * 3,
        grid_spec=pltpu.PrefetchScalarGridSpec(
            num_scalar_prefetch=1,
            grid=(count,),
            in_specs=in_specs,
            out_specs=[pl.BlockSpec((ROWS, 256), whole)] * 3,
        ),
        compiler_params=pltpu.CompilerParams(vmem_limit_bytes=24 << 20),
        cost_estimate=pl.CostEstimate(
            flops=2 * ROWS * BLOCK * 768 * count,
            bytes_accessed=count * 1024 * 1024 + 3 * 262144,
            transcendentals=0,
        ),
        name="partial_sums",
    )(rows, *blocks, *weights, *given)


def rotate_kernel(core_ref, q_ref, kv_ref, got_ref, cos_ref, sin_ref, tag_ref, query_ref, fresh_ref, page_ref):
    cosine, sine = cos_ref[...], sin_ref[...]

    def rotated(v):
        return v * cosine + pltpu.roll(v, HD // 2, 1) * sine

    for h in range(2):
        at = slice(h * HD, (h + 1) * HD)
        query = q_ref[:, at] + got_ref[:, at]
        query_ref[h * ROWS : (h + 1) * ROWS, :] = (rotated(query) * HD**-0.5).astype(BF)
    key = rotated(kv_ref[:, :HD] + got_ref[:, 256 : 256 + HD]).astype(BF)
    value = (kv_ref[:, HD:] + got_ref[:, 256 + HD :]).astype(BF)
    fresh_ref[:, :HD] = key
    fresh_ref[:, HD:] = value
    page_ref[0:ROWS, :] = jnp.where(core_ref[0] == 0, key.astype(F32), value.astype(F32)).astype(BF)
    page_ref[ROWS:, :] = tag_ref[...]


def attend_kernel(len_ref, query_ref, fresh_ref, cache_ref, out_ref):
    queries = query_ref[...]
    contract = (((1,), (1,)), ((), ()))
    old = lax.dot_general(queries, cache_ref[:, :HD], contract, preferred_element_type=F32)
    new = lax.dot_general(queries, fresh_ref[:, :HD], contract, preferred_element_type=F32)
    column = lax.broadcasted_iota(jnp.int32, old.shape, 1)
    old = jnp.where(column < len_ref[0], old, -jnp.inf)
    token = lax.broadcasted_iota(jnp.int32, new.shape, 0) & (ROWS - 1)
    column = lax.broadcasted_iota(jnp.int32, new.shape, 1)
    new = jnp.where(column <= token, new, -jnp.inf)
    highest = jnp.maximum(
        jnp.max(old, axis=1, keepdims=True), jnp.max(new, axis=1, keepdims=True)
    )
    old = jnp.exp(old - highest)
    new = jnp.exp(new - highest)
    total = jnp.sum(old, axis=1, keepdims=True) + jnp.sum(new, axis=1, keepdims=True)
    mixed = jnp.dot(old.astype(BF), cache_ref[:, HD:], preferred_element_type=F32)
    mixed += jnp.dot(new.astype(BF), fresh_ref[:, HD:], preferred_element_type=F32)
    result = (mixed / total).astype(BF)
    out_ref[:, :HD] = result[:ROWS]
    out_ref[:, HD:] = result[ROWS:]


def pack_kernel(own_ref, tag_ref, got_ref, out_ref):
    lane = lax.broadcasted_iota(jnp.int32, (1, ROWS), 1)
    within = lax.rem(lane, PAGE)
    rows = out_ref.shape[0]
    row = lax.broadcasted_iota(jnp.int32, (rows, ROWS), 0)

    def placed(tags):
        slots = tags.astype(F32).astype(jnp.int32)
        hit = None
        for copy in range(2):
            slot = jnp.concatenate([slots[2 * copy : 2 * copy + 1], slots[2 * copy + 1 : 2 * copy + 2]], axis=1)
            same = row == slot * PAGE + within
            hit = same if hit is None else hit | same
        return jnp.where(hit, 1.0, 0.0).astype(BF)

    out = jnp.dot(placed(tag_ref[...]), own_ref[0:ROWS, :], preferred_element_type=F32)
    out += jnp.dot(placed(got_ref[ROWS:, :]), got_ref[0:ROWS, :], preferred_element_type=F32)
    out_ref[...] = out.astype(BF)


def shards(tokens, w_query, w_keyval, prefix_cache, prefix_len, page_owner):
    place = lax.axis_index("tp")
    row = lax.axis_index("row")
    chip, core = place // 2, place % 2
    half, pages = row // 16, page_owner.shape[0]
    siblings = [(t, t ^ 1) for t in range(2 * CHIPS)]

    mine = lax.all_gather(
        tokens, "tp", axis=0, tiled=True,
        axis_index_groups=[[2 * c, 2 * c + 1] for c in range(CHIPS)],
    )
    held = {0: mine}
    for got, had in STEPS:
        held[got] = lax.ppermute(held[had], "tp", step_perm(got, had))
    w_other = lax.ppermute(w_query, "tp", siblings)

    inverse = ROPE_BASE ** (-(jnp.arange(HD // 2, dtype=F32) * 2.0 / HD))
    positions = prefix_len[0].astype(F32) + jnp.arange(ROWS, dtype=F32)
    angles = positions[:, None] * inverse
    cosine, sine = jnp.cos(angles), jnp.sin(angles)
    cosine = jnp.concatenate([cosine, cosine], axis=1)
    sine = jnp.concatenate([-sine, sine], axis=1)
    owner = page_owner.reshape(-1)
    same = owner[:, None] == owner[None, :]
    earlier = jnp.arange(2 * pages)[None, :] < jnp.arange(2 * pages)[:, None]
    rank = jnp.sum((same & earlier).astype(jnp.int32), axis=1)
    slot = (owner % 16) * 4 + half * 2 + rank

    def tags(target):
        kept = jnp.where(owner // 16 == target, slot, 128).reshape(pages, 2)
        lanes = jnp.repeat(kept.T, PAGE, axis=1).reshape(4, HD)
        return jnp.concatenate([lanes, jnp.full((12, HD), 128, jnp.int32)], axis=0).astype(BF)

    own_tags, sent_tags = tags(half), tags(1 - half)

    def block_of(offset):
        return jnp.clip(jnp.where(core == 0, chip - offset, chip + offset), 0, CHIPS - 1)

    early = jnp.stack([block_of(k) for k in EARLY] + [place]).astype(jnp.int32)
    late = jnp.stack([block_of(k) for k in LATE]).astype(jnp.int32)
    weights = [w_query, w_other, w_keyval]
    sums = partial_sums(early, [held[k] for k in EARLY], weights, tokens, True)
    query, other, keyval = partial_sums(late, [held[k] for k in LATE], weights, sums, False)
    got = lax.ppermute(jnp.concatenate([other, keyval], axis=1), "tp", siblings)

    queries, fresh, page = pl.pallas_call(
        rotate_kernel,
        out_shape=[
            jax.ShapeDtypeStruct((2 * ROWS, HD), BF),
            jax.ShapeDtypeStruct((ROWS, 2 * HD), BF),
            jax.ShapeDtypeStruct((ROWS + 16, HD), BF),
        ],
        in_specs=[pl.BlockSpec(memory_space=pltpu.SMEM)] + [pl.BlockSpec()] * 6,
        name="rotate",
    )(core.reshape(1).astype(jnp.int32), query, keyval, got, cosine, sine, sent_tags)

    far = lax.ppermute(page, "row", [(r, (r + 16) % 32) for r in range(32)])
    context = pl.pallas_call(
        attend_kernel,
        out_shape=jax.ShapeDtypeStruct((ROWS, 2 * HD), BF),
        in_specs=[pl.BlockSpec(memory_space=pltpu.SMEM)] + [pl.BlockSpec()] * 3,
        compiler_params=pltpu.CompilerParams(vmem_limit_bytes=40 << 20),
        cost_estimate=pl.CostEstimate(flops=400_000_000, bytes_accessed=1_000_000, transcendentals=700_000),
        name="attend",
    )(prefix_len, queries, fresh, prefix_cache[0])
    packed = pl.pallas_call(
        pack_kernel,
        out_shape=jax.ShapeDtypeStruct((64 * PAGE, HD), BF),
        compiler_params=pltpu.CompilerParams(vmem_limit_bytes=24 << 20),
        name="pack",
    )(page, own_tags, far)
    received = lax.all_to_all(
        packed, "row", 0, 0, tiled=True,
        axis_index_groups=[[z * 16 + i for i in range(16)] for z in range(2)],
    )
    store = received.reshape(16, 2, 2, PAGE, HD).transpose(1, 0, 2, 3, 4)
    return context, store.reshape(64, PAGE, HD)


def solution(mesh):
    return jax.shard_map(
        shards,
        mesh=mesh,
        in_specs=(
            P("row", "tp"),
            P(None, "tp"),
            P(None, "tp"),
            P("row", None, "tp"),
            P("row"),
            P("row", None),
        ),
        out_specs=(P("row", "tp"), P("row", None, "tp")),
        check_vma=False,
    )
```

time: 158 us -> 100 us (0.63)
  the two profiles are of different devices: /device:TPU:2 before, /device:TPU:160 now
where the time goes in v1:
time: 100 us; the launch traced here: 99.3 us
  starting transfers between devices  36.9 us (37%)
  waiting for transfers between devices  31.3 us (31%)
  Pallas kernels  12.1 us (12%)
  local copies, waits for them, and re-layouts  11.1 us (11%)
  blocking collectives  4.52 us (5%)
  other arithmetic  1.7 us (2%)
  between operations  1.6 us (2%)
    ppermute x7, starting transfers between devices, shards(): held[got] = lax.ppermute(held[had], 'tp', step_perm(got, had))  19.6 us
    ppermute x7, waiting for transfers between devices, shards(): held[got] = lax.ppermute(held[had], 'tp', step_perm(got, had))  15.1 us
    ppermute x1, waiting for transfers between devices, shards(): far = lax.ppermute(page, 'row', [(r, (r + 16) % 32) for r in range(32)])  11.5 us
    unnamed x25, local copies, waits for them, and re-layouts  9.05 us
    all_to_all x1, starting transfers between devices, shards(): lax.all_to_all(packed, 'row', 0, 0, tiled=True, axis_index_groups=[[z * 1...  7.04 us
    pallas_call x2, Pallas kernels, partial_sums(): pl.pallas_call(functools.partial(partial_kernel, count, first), out_shape...  6.26 us
    ppermute x1, starting transfers between devices, shards(): far = lax.ppermute(page, 'row', [(r, (r + 16) % 32) for r in range(32)])  6.26 us
    all_gather x1, blocking collectives, shards(): lax.all_gather(tokens, 'tp', axis=0, tiled=True, axis_index_groups=[[2 *...  4.52 us
  transfers between devices with their start and end apart: 11, of which 5 were waited for; matrix products, arithmetic and copies ran while one was open for 4% of the time, Pallas kernels for 6%

profile of v1, /device:TPU:160, one launch (start us, length us, event | category | flops | bytes accessed | tf_op | source)
XLA Modules:
  0.0 99.3 jit_solution(17477406262589398981)
XLA Ops:
  0.6 1.9 %collective-permute-start.5 = (bf16[4096,256]{1,0:T(8,128)(2,1)}, bf16[4096,256]{1,0:T(8,128)(2,1)S(1)}, u32[]{:S(2)}, u32[]{:S(2)}) collective-permute-start(bf16[4096,256]{1,0:T(8,128)(2,1)} %refs_3_.1), channel_id=1, source_target_pairs={{0,1},{1,0},{2,3},{3,2},{4,5},{5,4},{6,7},{7,6},{8,9},{9,8},{10,11... | collective-permute-start | bytes 6291464 | tf_op jit(solution)/shard_map/ppermute | solution.py:164
  2.6 4.5 %all_gather.3 = bf16[512,256]{1,0:T(8,128)(2,1)S(1)} all-gather(bf16[256,256]{1,0:T(8,128)(2,1)} %refs_7_.1), channel_id=1, replica_groups={{0,1},{2,3},{4,5},{6,7},{8,9},{10,11},{12,13},{14,15},{16,17},{18,19},{..., dimensions={0}, use_global_device_ids=true | all-gather | bytes 393216 | tf_op jit(solution)/shard_map/all_gather | solution.py:157
  7.1 1.3 %collective-permute-start = (bf16[512,256]{1,0:T(8,128)(2,1)S(1)}, bf16[512,256]{1,0:T(8,128)(2,1)S(1)}, u32[]{:S(2)}, u32[]{:S(2)}) collective-permute-start(bf16[512,256]{1,0:T(8,128)(2,1)S(1)} %all_gather.3), channel_id=1, source_target_pairs={{0,6},{2,8},{4,10},{6,12},{8,14},{7,1},{9,3},{11,5},{13,7},{15,9},... | collective-permute-start | bytes 786440 | tf_op jit(solution)/shard_map/ppermute | solution.py:163
  8.4 3.8 %collective-permute-start.6 = (bf16[512,256]{1,0:T(8,128)(2,1)S(1)}, bf16[512,256]{1,0:T(8,128)(2,1)S(1)}, u32[]{:S(2)}, u32[]{:S(2)}) collective-permute-start(bf16[512,256]{1,0:T(8,128)(2,1)S(1)} %all_gather.3), channel_id=1, source_target_pairs={{0,2},{2,4},{4,6},{6,8},{8,10},{10,12},{12,14},{3,1},{5,3},{7,5},{... | collective-permute-start | bytes 786440 | tf_op jit(solution)/shard_map/ppermute | solution.py:163
  12.2 10.0 %collective-permute-done.refs_2_ = bf16[512,256]{1,0:T(8,128)(2,1)S(1)} collective-permute-done((bf16[512,256]{1,0:T(8,128)(2,1)S(1)}, bf16[512,256]{1,0:T(8,128)(2,1)S(1)}, u32[]{:S(2)}, u32[]{:S(2)}) %collective-permute-start) | collective-permute-done | bytes 262176 | tf_op jit(solution)/shard_map/ppermute | solution.py:163
  22.2 5.6 %collective-permute-start.1 = (bf16[512,256]{1,0:T(8,128)(2,1)S(1)}, bf16[512,256]{1,0:T(8,128)(2,1)S(1)}, u32[]{:S(2)}, u32[]{:S(2)}) collective-permute-start(bf16[512,256]{1,0:T(8,128)(2,1)S(1)} %collective-permute-done.refs_2_), channel_id=1, source_target_pairs={{6,8},{8,10},{10,12},{12,14},{3,1},{5,3},{7,5},{9,7},{22,24},{24,2... | collective-permute-start | bytes 786440 | tf_op jit(solution)/shard_map/ppermute | solution.py:163
  27.8 0.7 collective-permute-start.3
  28.5 0.8 copy.24
  29.2 0.1 eq.45
  29.3 0.2 convert_reduce_fusion
  29.5 0.1 reduce_sum.12
  29.6 0.0 collective-permute-done.6.refs_0_
  29.6 2.5 %collective-permute-start.7 = (bf16[512,256]{1,0:T(8,128)(2,1)S(1)}, bf16[512,256]{1,0:T(8,128)(2,1)}, u32[]{:S(2)}, u32[]{:S(2)}) collective-permute-start(bf16[512,256]{1,0:T(8,128)(2,1)S(1)} %collective-permute-done.6.refs_0_), channel_id=1, source_target_pairs={{2,4},{4,6},{6,8},{8,10},{10,12},{12,14},{3,1},{5,3},{7,5},{9,7},{... | collective-permute-start | bytes 786440 | tf_op jit(solution)/shard_map/ppermute | solution.py:163
  32.1 5.1 %collective-permute-done.1.refs_3_ = bf16[512,256]{1,0:T(8,128)(2,1)S(1)} collective-permute-done((bf16[512,256]{1,0:T(8,128)(2,1)S(1)}, bf16[512,256]{1,0:T(8,128)(2,1)S(1)}, u32[]{:S(2)}, u32[]{:S(2)}) %collective-permute-start.1) | collective-permute-done | bytes 262176 | tf_op jit(solution)/shard_map/ppermute | solution.py:163
  37.3 4.3 %collective-permute-start.2 = (bf16[512,256]{1,0:T(8,128)(2,1)S(1)}, bf16[512,256]{1,0:T(8,128)(2,1)S(1)}, u32[]{:S(2)}, u32[]{:S(2)}) collective-permute-start(bf16[512,256]{1,0:T(8,128)(2,1)S(1)} %collective-permute-done.1.refs_3_), channel_id=1, source_target_pairs={{8,10},{10,12},{12,14},{3,1},{5,3},{7,5},{24,26},{26,28},{28,30},{... | collective-permute-start | bytes 786440 | tf_op jit(solution)/shard_map/ppermute | solution.py:163
  41.7 1.4 %collective-permute-start.4 = (bf16[512,256]{1,0:T(8,128)(2,1)S(1)}, bf16[512,256]{1,0:T(8,128)(2,1)}, u32[]{:S(2)}, u32[]{:S(2)}) collective-permute-start(bf16[512,256]{1,0:T(8,128)(2,1)S(1)} %collective-permute-done.3.refs_1_), channel_id=1, source_target_pairs={{12,14},{3,1},{28,30},{19,17},{44,46},{35,33},{60,62},{51,49},{76,... | collective-permute-start | bytes 786440 | tf_op jit(solution)/shard_map/ppermute | solution.py:163
  43.1 0.1 copy.29
  43.2 0.1 broadcast_in_dim.16
  43.3 0.1 reshape_reshape.8
  44.0 0.6 concatenate.18.tag_ref
  44.6 0.1 stack.39.rows_ref
  44.7 0.1 pad_add_fusion.rows_ref
  44.8 1.6 %copy-done = bf16[4096,256]{1,0:T(8,128)(2,1)S(1)} copy-done((bf16[4096,256]{1,0:T(8,128)(2,1)S(1)}, bf16[4096,256]{1,0:T(8,128)(2,1)}, u32[]{:S(2)}) %copy-start) | copy-done | bytes 2097176
  46.4 1.6 %copy-done.2 = bf16[4096,256]{1,0:T(8,128)(2,1)S(1)} copy-done((bf16[4096,256]{1,0:T(8,128)(2,1)S(1)}, bf16[4096,256]{1,0:T(8,128)(2,1)}, u32[]{:S(2)}) %copy-start.2) | copy-done | bytes 2097176
  48.0 0.9 copy-done.5
  48.9 3.5 %partial_sums.2 = (f32[256,256]{1,0:T(8,128)S(1)}, f32[256,256]{1,0:T(8,128)S(1)}, f32[256,256]{1,0:T(8,128)S(1)}) custom-call(s32[5]{0:T(128)S(1)} %stack.39.rows_ref, bf16[512,256]{1,0:T(8,128)(2,1)S(1)} %collective-permute-done.6.refs_0_, bf16[512,256]{1,0:T(8,128)(2,1)} %collective-permute-done.7.refs_1_, ...), custom_call_target="tpu_custom_call" | custom-call | flops 805306368 | bytes 4980736 | tf_op jit(solution)/shard_map/partial_sums/pallas_call | solution.py:70
  52.5 2.7 %partial_sums.3 = (f32[256,256]{1,0:T(8,128)S(1)}, f32[256,256]{1,0:T(8,128)S(1)}, f32[256,256]{1,0:T(8,128)S(1)}) custom-call(s32[3]{0:T(128)S(1)} %pad_add_fusion.rows_ref, bf16[512,256]{1,0:T(8,128)(2,1)S(1)} %collective-permute-done.2.refs_0_, bf16[512,256]{1,0:T(8,128)(2,1)S(1)} %collective-permute-done.3.refs_1_, ...), custom_call_target="tpu_custom_call" | custom-call | flops 603979776 | bytes 3932160 | tf_op jit(solution)/shard_map/partial_sums/pallas_call | solution.py:70
  55.2 0.7 copy-done.6
  55.9 0.1 pad_maximum_fusion
  56.0 2.1 %collective-permute-start.8 = (f32[256,512]{1,0:T(8,128)S(1)}, f32[256,512]{1,0:T(8,128)S(1)}, u32[]{:S(2)}, u32[]{:S(2)}) collective-permute-start(f32[256,512]{1,0:T(8,128)S(1)} %pad_maximum_fusion), channel_id=1, source_target_pairs={{0,1},{1,0},{2,3},{3,2},{4,5},{5,4},{6,7},{7,6},{8,9},{9,8},{10,11... | collective-permute-start | bytes 1572872 | tf_op jit(solution)/shard_map/ppermute | solution.py:193
  58.1 0.5 fusion
  58.6 0.8 pad_maximum_fusion.1
  59.4 0.5 collective-permute-done.8.got_ref
  59.9 0.8 copy-done.11
  60.7 2.2 %rotate.1 = (bf16[512,128]{1,0:T(8,128)(2,1)}, bf16[256,256]{1,0:T(8,128)(2,1)}, bf16[272,128]{1,0:T(8,128)(2,1)}) custom-call(s32[1]{0:T(128)} %bitcast.core_ref, f32[256,256]{1,0:T(8,128)} %copy-done.6, f32[256,256]{1,0:T(8,128)} %copy-done.4, f32[256,512]{1,0:T(8,128)} %copy-done.11, f32[256,128]{1,0:T(8,128)} %get-tuple-element.25.cos_ref, ...), custom_call_target="tpu_custom_call" | custom-call | tf_op jit(solution)/shard_map/rotate/pallas_call | solution.py:195
  62.9 6.3 %collective-permute-start.9 = (bf16[272,128]{1,0:T(8,128)(2,1)}, bf16[272,128]{1,0:T(8,128)(2,1)S(1)}, u32[]{:S(2)}, u32[]{:S(2)}) collective-permute-start(bf16[272,128]{1,0:T(8,128)(2,1)} %get-tuple-element.19.own_ref), channel_id=1, source_target_pairs={{0,256},{16,272},{32,288},{48,304},{64,320},{80,336},{96,352},{112... | collective-permute-start | bytes 208904 | tf_op jit(solution)/shard_map/ppermute | solution.py:206
  69.1 0.1 copy.30
  69.2 0.1 broadcast_in_dim.17
  69.3 0.1 reshape_reshape.9
  69.4 11.5 %collective-permute-done.9.got_ref = bf16[272,128]{1,0:T(8,128)(2,1)S(1)} collective-permute-done((bf16[272,128]{1,0:T(8,128)(2,1)}, bf16[272,128]{1,0:T(8,128)(2,1)S(1)}, u32[]{:S(2)}, u32[]{:S(2)}) %collective-permute-start.9) | collective-permute-done | bytes 69664 | tf_op jit(solution)/shard_map/ppermute | solution.py:206
  80.9 0.9 copy-done.7
  81.8 1.3 %pack.1 = bf16[1024,128]{1,0:T(8,128)(2,1)} custom-call(bf16[272,128]{1,0:T(8,128)(2,1)S(1)} %copy-done.7, bf16[16,128]{1,0:T(8,128)(2,1)S(1)} %concatenate.19.tag_ref, bf16[272,128]{1,0:T(8,128)(2,1)S(1)} %collective-permute-done.9.got_ref), custom_call_target="tpu_custom_call" | custom-call | tf_op jit(solution)/shard_map/pack/pallas_call | solution.py:215
  83.0 7.0 %all-to-all-start = ((bf16[16,64,128]{2,1,0:T(8,128)(2,1)}), bf16[16,64,128]{2,1,0:T(8,128)(2,1)S(1)}, u32[]{:S(2)}, u32[]{:S(2)}) async-start(bf16[16,64,128]{2,1,0:T(8,128)(2,1)} %bitcast.13), calls=%async_computation | async-start | bytes 524288 | tf_op jit(solution)/shard_map/all_to_all | solution.py:221
  90.1 0.9 copy-done.9
  91.0 0.9 copy-done.10
  91.9 2.5 %attend.1 = bf16[256,256]{1,0:T(8,128)(2,1)} custom-call(s32[1]{0:T(128)S(6)} %copy.32.len_ref, bf16[512,128]{1,0:T(8,128)(2,1)S(1)} %copy-done.9, bf16[256,256]{1,0:T(8,128)(2,1)S(1)} %copy-done.10, bf16[1024,256]{1,0:T(8,128)(2,1)S(1)} %bitcast.20), custom_call_target="tpu_custom_call" | custom-call | flops 400000000 | bytes 1000000 | tf_op jit(solution)/shard_map/attend/pallas_call | solution.py:207
  94.4 4.2 %all-to-all-done = bf16[16,64,128]{2,1,0:T(8,128)(2,1)S(1)} async-done(((bf16[16,64,128]{2,1,0:T(8,128)(2,1)}), bf16[16,64,128]{2,1,0:T(8,128)(2,1)S(1)}, u32[]{:S(2)}, u32[]{:S(2)}) %all-to-all-start) | async-done | bytes 262176 | tf_op jit(solution)/shard_map/all_to_all | solution.py:221
  98.6 0.7 copy.31
  (25 shorter events, 0.1 us)
Async XLA Ops:
  0.6 44.2 %collective-permute-start.5 = (bf16[4096,256]{1,0:T(8,128)(2,1)}, bf16[4096,256]{1,0:T(8,128)(2,1)S(1)}, u32[]{:S(2)}, u32[]{:S(2)}) collective-permute-start(bf16[4096,256]{1,0:T(8,128)(2,1)} %refs_3_.1), channel_id=1, source_target_pairs={{0,1},{1,0},{2,3},{3,2},{4,5},{5,4},{6,7},{7,6},{8,9},{9,8},{10,11... | collective-permute-start | bytes 6291464 | tf_op jit(solution)/shard_map/ppermute | solution.py:164
  7.1 15.1 %collective-permute-start = (bf16[512,256]{1,0:T(8,128)(2,1)S(1)}, bf16[512,256]{1,0:T(8,128)(2,1)S(1)}, u32[]{:S(2)}, u32[]{:S(2)}) collective-permute-start(bf16[512,256]{1,0:T(8,128)(2,1)S(1)} %all_gather.3), channel_id=1, source_target_pairs={{0,6},{2,8},{4,10},{6,12},{8,14},{7,1},{9,3},{11,5},{13,7},{15,9},... | collective-permute-start | bytes 786440 | tf_op jit(solution)/shard_map/ppermute | solution.py:163
  8.4 21.2 %collective-permute-start.6 = (bf16[512,256]{1,0:T(8,128)(2,1)S(1)}, bf16[512,256]{1,0:T(8,128)(2,1)S(1)}, u32[]{:S(2)}, u32[]{:S(2)}) collective-permute-start(bf16[512,256]{1,0:T(8,128)(2,1)S(1)} %all_gather.3), channel_id=1, source_target_pairs={{0,2},{2,4},{4,6},{6,8},{8,10},{10,12},{12,14},{3,1},{5,3},{7,5},{... | collective-permute-start | bytes 786440 | tf_op jit(solution)/shard_map/ppermute | solution.py:163
  22.2 15.1 %collective-permute-start.1 = (bf16[512,256]{1,0:T(8,128)(2,1)S(1)}, bf16[512,256]{1,0:T(8,128)(2,1)S(1)}, u32[]{:S(2)}, u32[]{:S(2)}) collective-permute-start(bf16[512,256]{1,0:T(8,128)(2,1)S(1)} %collective-permute-done.refs_2_), channel_id=1, source_target_pairs={{6,8},{8,10},{10,12},{12,14},{3,1},{5,3},{7,5},{9,7},{22,24},{24,2... | collective-permute-start | bytes 786440 | tf_op jit(solution)/shard_map/ppermute | solution.py:163
  27.8 13.9 %collective-permute-start.3 = (bf16[512,256]{1,0:T(8,128)(2,1)S(1)}, bf16[512,256]{1,0:T(8,128)(2,1)S(1)}, u32[]{:S(2)}, u32[]{:S(2)}) collective-permute-start(bf16[512,256]{1,0:T(8,128)(2,1)S(1)} %collective-permute-done.refs_2_), channel_id=1, source_target_pairs={{6,12},{8,14},{7,1},{9,3},{22,28},{24,30},{23,17},{25,19},{38,44},... | collective-permute-start | bytes 786440 | tf_op jit(solution)/shard_map/ppermute | solution.py:163
  29.6 15.2 %collective-permute-start.7 = (bf16[512,256]{1,0:T(8,128)(2,1)S(1)}, bf16[512,256]{1,0:T(8,128)(2,1)}, u32[]{:S(2)}, u32[]{:S(2)}) collective-permute-start(bf16[512,256]{1,0:T(8,128)(2,1)S(1)} %collective-permute-done.6.refs_0_), channel_id=1, source_target_pairs={{2,4},{4,6},{6,8},{8,10},{10,12},{12,14},{3,1},{5,3},{7,5},{9,7},{... | collective-permute-start | bytes 786440 | tf_op jit(solution)/shard_map/ppermute | solution.py:163
  37.3 15.1 %collective-permute-start.2 = (bf16[512,256]{1,0:T(8,128)(2,1)S(1)}, bf16[512,256]{1,0:T(8,128)(2,1)S(1)}, u32[]{:S(2)}, u32[]{:S(2)}) collective-permute-start(bf16[512,256]{1,0:T(8,128)(2,1)S(1)} %collective-permute-done.1.refs_3_), channel_id=1, source_target_pairs={{8,10},{10,12},{12,14},{3,1},{5,3},{7,5},{24,26},{26,28},{28,30},{... | collective-permute-start | bytes 786440 | tf_op jit(solution)/shard_map/ppermute | solution.py:163
  41.7 10.8 %collective-permute-start.4 = (bf16[512,256]{1,0:T(8,128)(2,1)S(1)}, bf16[512,256]{1,0:T(8,128)(2,1)}, u32[]{:S(2)}, u32[]{:S(2)}) collective-permute-start(bf16[512,256]{1,0:T(8,128)(2,1)S(1)} %collective-permute-done.3.refs_1_), channel_id=1, source_target_pairs={{12,14},{3,1},{28,30},{19,17},{44,46},{35,33},{60,62},{51,49},{76,... | collective-permute-start | bytes 786440 | tf_op jit(solution)/shard_map/ppermute | solution.py:163
  44.8 1.6 %copy-start = (bf16[4096,256]{1,0:T(8,128)(2,1)S(1)}, bf16[4096,256]{1,0:T(8,128)(2,1)}, u32[]{:S(2)}) copy-start(bf16[4096,256]{1,0:T(8,128)(2,1)} %refs_3_.1) | copy-start | bytes 6291460
  46.4 1.6 %copy-start.2 = (bf16[4096,256]{1,0:T(8,128)(2,1)S(1)}, bf16[4096,256]{1,0:T(8,128)(2,1)}, u32[]{:S(2)}) copy-start(bf16[4096,256]{1,0:T(8,128)(2,1)} %refs_5_.1) | copy-start | bytes 6291460
  48.0 0.9 copy-start.5
  48.9 3.6 %copy-start.1 = (bf16[4096,256]{1,0:T(8,128)(2,1)S(1)}, bf16[4096,256]{1,0:T(8,128)(2,1)}, u32[]{:S(2)}) copy-start(bf16[4096,256]{1,0:T(8,128)(2,1)} %refs_3_.1) | copy-start | bytes 6291460
  48.9 3.6 %copy-start.3 = (bf16[4096,256]{1,0:T(8,128)(2,1)S(1)}, bf16[4096,256]{1,0:T(8,128)(2,1)}, u32[]{:S(2)}) copy-start(bf16[4096,256]{1,0:T(8,128)(2,1)} %refs_5_.1) | copy-start | bytes 6291460
  55.2 0.7 copy-start.6
  55.9 4.0 %copy-start.4 = (f32[256,256]{1,0:T(8,128)}, f32[256,256]{1,0:T(8,128)S(1)}, u32[]{:S(2)}) copy-start(f32[256,256]{1,0:T(8,128)S(1)} %get-tuple-element.15.kv_ref) | copy-start | bytes 786436
  55.9 34.2 %copy-start.8 = (bf16[1,1024,256]{2,1,0:T(8,128)(2,1)S(1)}, bf16[1,1024,256]{2,1,0:T(8,128)(2,1)}, u32[]{:S(2)}) copy-start(bf16[1,1024,256]{2,1,0:T(8,128)(2,1)} %param.9) | copy-start | bytes 1572868
  56.0 3.9 %collective-permute-start.8 = (f32[256,512]{1,0:T(8,128)S(1)}, f32[256,512]{1,0:T(8,128)S(1)}, u32[]{:S(2)}, u32[]{:S(2)}) collective-permute-start(f32[256,512]{1,0:T(8,128)S(1)} %pad_maximum_fusion), channel_id=1, source_target_pairs={{0,1},{1,0},{2,3},{3,2},{4,5},{5,4},{6,7},{7,6},{8,9},{9,8},{10,11... | collective-permute-start | bytes 1572872 | tf_op jit(solution)/shard_map/ppermute | solution.py:193
  59.9 0.8 copy-start.11
  62.9 18.0 %collective-permute-start.9 = (bf16[272,128]{1,0:T(8,128)(2,1)}, bf16[272,128]{1,0:T(8,128)(2,1)S(1)}, u32[]{:S(2)}, u32[]{:S(2)}) collective-permute-start(bf16[272,128]{1,0:T(8,128)(2,1)} %get-tuple-element.19.own_ref), channel_id=1, source_target_pairs={{0,256},{16,272},{32,288},{48,304},{64,320},{80,336},{96,352},{112... | collective-permute-start | bytes 208904 | tf_op jit(solution)/shard_map/ppermute | solution.py:206
  80.9 0.9 copy-start.7
  83.0 15.5 %all-to-all-start = ((bf16[16,64,128]{2,1,0:T(8,128)(2,1)}), bf16[16,64,128]{2,1,0:T(8,128)(2,1)S(1)}, u32[]{:S(2)}, u32[]{:S(2)}) async-start(bf16[16,64,128]{2,1,0:T(8,128)(2,1)} %bitcast.13), calls=%async_computation | async-start | bytes 524288 | tf_op jit(solution)/shard_map/all_to_all | solution.py:221
  90.1 0.9 copy-start.9
  91.0 0.9 copy-start.10

commit v2 on v1

--- a/solution.py
+++ b/solution.py
@@ -12,9 +12,8 @@
 CHIPS = 8
 ROWS = 256
 BLOCK = 512
-STEPS = ((3, 0), (1, 0), (2, 1), (4, 3), (6, 3), (5, 4), (7, 6))
-EARLY = (1, 2, 3, 4)
-LATE = (5, 6, 7)
+VMEM = pl.BlockSpec(memory_space=pltpu.VMEM)
+SMEM = pl.BlockSpec(memory_space=pltpu.SMEM)
 BF = jnp.bfloat16
 F32 = jnp.float32
 
@@ -28,65 +27,51 @@
     return right + left
 
 
-def partial_kernel(count, first, rows_ref, *refs):
-    blocks, refs = refs[:count], refs[count:]
-    weights, refs = refs[:3], refs[3:]
-    given, outs = refs[: len(refs) - 3], refs[len(refs) - 3 :]
-    step = pl.program_id(0)
-
-    def add(block):
-        for j in range(3):
-            product = jnp.dot(block[0:ROWS], weights[j][0:256], preferred_element_type=F32)
-            product += jnp.dot(block[ROWS:], weights[j][256:], preferred_element_type=F32)
-            outs[j][...] += product
-
-    @pl.when(step == 0)
-    def _():
-        if first:
-            own, given_weights = given[0], given[1:]
-            for j in range(3):
-                outs[j][...] = jnp.dot(
-                    own[...], given_weights[j][...], preferred_element_type=F32
-                )
-        else:
-            for j in range(3):
-                outs[j][...] = given[j][...]
-
-    for s in range(count):
-        pl.when(step == s)(functools.partial(add, blocks[s]))
-
-
-def partial_sums(rows, blocks, weights, given, first):
-    count = len(blocks)
-    whole = lambda s, r: (0, 0)
-    in_specs = [pl.BlockSpec((2 * ROWS, 256), whole)] * count
-    in_specs += [pl.BlockSpec((BLOCK, 256), lambda s, r: (r[s], 0))] * 3
-    if first:
-        in_specs += [pl.BlockSpec((ROWS, 256), whole)]
-        in_specs += [pl.BlockSpec((256, 256), lambda s, r: (r[count], 0))] * 3
-        given = [given] + list(weights)
+def partial_kernel(offsets, own, rows_ref, *refs):
+    count = len(offsets)
+    blocks, weights, refs = refs[:count], refs[count : count + 3], refs[count + 3 :]
+    given, (keep_ref, send_ref) = refs[:-2], refs[-2:]
+
+    def terms(block, start, depth):
+        at = pl.ds(pl.multiple_of(start, depth), depth)
+        return [jnp.dot(block, w[at, :], preferred_element_type=F32) for w in weights]
+
+    if own:
+        sums = terms(given[0][...], rows_ref[0] * ROWS, ROWS)
     else:
-        in_specs += [pl.BlockSpec((ROWS, 256), whole)] * 3
+        sums = [given[0][...], given[1][:, :256], given[1][:, 256:]]
+    for block, offset in zip(blocks, offsets):
+        both = jnp.concatenate([block[:ROWS], block[ROWS:]], axis=1)
+        found = terms(both, rows_ref[offset] * BLOCK, BLOCK)
+        sums = [x + y for x, y in zip(sums, found)]
+    keep_ref[...] = sums[0]
+    send_ref[:, :256] = sums[1]
+    send_ref[:, 256:] = sums[2]
+
+
+def partial_sums(rows, offsets, blocks, weights, given, own):
+    operands = [*blocks, *weights, *given]
     return pl.pallas_call(
-        functools.partial(partial_kernel, count, first),
-        out_shape=[jax.ShapeDtypeStruct((ROWS, 256), F32)] * 3,
-        grid_spec=pltpu.PrefetchScalarGridSpec(
-            num_scalar_prefetch=1,
-            grid=(count,),
-            in_specs=in_specs,
-            out_specs=[pl.BlockSpec((ROWS, 256), whole)] * 3,
-        ),
-        compiler_params=pltpu.CompilerParams(vmem_limit_bytes=24 << 20),
+        functools.partial(partial_kernel, offsets, own),
+        out_shape=[
+            jax.ShapeDtypeStruct((ROWS, 256), F32),
+            jax.ShapeDtypeStruct((ROWS, 512), F32),
+        ],
+        in_specs=[SMEM] + [VMEM] * len(operands),
+        out_specs=[VMEM] * 2,
+        compiler_params=pltpu.CompilerParams(vmem_limit_bytes=16 << 20),
         cost_estimate=pl.CostEstimate(
-            flops=2 * ROWS * BLOCK * 768 * count,
-            bytes_accessed=count * 1024 * 1024 + 3 * 262144,
+            flops=2 * ROWS * BLOCK * 768 * len(offsets),
+            bytes_accessed=len(offsets) * 1024 * 1024,
             transcendentals=0,
         ),
         name="partial_sums",
-    )(rows, *blocks, *weights, *given)
-
-
-def rotate_kernel(core_ref, q_ref, kv_ref, got_ref, cos_ref, sin_ref, tag_ref, query_ref, fresh_ref, page_ref):
+    )(rows, *operands)
+
+
+def rotate_kernel(
+    core_ref, q_ref, sent_ref, got_ref, cos_ref, sin_ref, tag_ref, query_ref, fresh_ref, page_ref
+):
     cosine, sine = cos_ref[...], sin_ref[...]
 
     def rotated(v):
@@ -96,8 +81,8 @@
         at = slice(h * HD, (h + 1) * HD)
         query = q_ref[:, at] + got_ref[:, at]
         query_ref[h * ROWS : (h + 1) * ROWS, :] = (rotated(query) * HD**-0.5).astype(BF)
-    key = rotated(kv_ref[:, :HD] + got_ref[:, 256 : 256 + HD]).astype(BF)
-    value = (kv_ref[:, HD:] + got_ref[:, 256 + HD :]).astype(BF)
+    key = rotated(sent_ref[:, 256 : 256 + HD] + got_ref[:, 256 : 256 + HD]).astype(BF)
+    value = (sent_ref[:, 256 + HD :] + got_ref[:, 256 + HD :]).astype(BF)
     fresh_ref[:, :HD] = key
     fresh_ref[:, HD:] = value
     page_ref[0:ROWS, :] = jnp.where(core_ref[0] == 0, key.astype(F32), value.astype(F32)).astype(BF)
@@ -158,11 +143,6 @@
         tokens, "tp", axis=0, tiled=True,
         axis_index_groups=[[2 * c, 2 * c + 1] for c in range(CHIPS)],
     )
-    held = {0: mine}
-    for got, had in STEPS:
-        held[got] = lax.ppermute(held[had], "tp", step_perm(got, had))
-    w_other = lax.ppermute(w_query, "tp", siblings)
-
     inverse = ROPE_BASE ** (-(jnp.arange(HD // 2, dtype=F32) * 2.0 / HD))
     positions = prefix_len[0].astype(F32) + jnp.arange(ROWS, dtype=F32)
     angles = positions[:, None] * inverse
@@ -185,12 +165,41 @@
     def block_of(offset):
         return jnp.clip(jnp.where(core == 0, chip - offset, chip + offset), 0, CHIPS - 1)
 
-    early = jnp.stack([block_of(k) for k in EARLY] + [place]).astype(jnp.int32)
-    late = jnp.stack([block_of(k) for k in LATE]).astype(jnp.int32)
-    weights = [w_query, w_other, w_keyval]
-    sums = partial_sums(early, [held[k] for k in EARLY], weights, tokens, True)
-    query, other, keyval = partial_sums(late, [held[k] for k in LATE], weights, sums, False)
-    got = lax.ppermute(jnp.concatenate([other, keyval], axis=1), "tp", siblings)
+    rows = jnp.stack([place] + [block_of(k) for k in range(1, CHIPS)]).astype(jnp.int32)
+    held = {0: mine}
+
+    def receive(got, had):
+        held[got] = lax.ppermute(held[had], "tp", step_perm(got, had))
+
+    w_sent, _ = lax.optimization_barrier((w_query, mine))
+    w_other = lax.ppermute(w_sent, "tp", siblings)
+    weights = [
+        pltpu.with_memory_space_constraint(w, pltpu.VMEM) for w in (w_query, w_other, w_keyval)
+    ]
+    receive(3, 0)
+    receive(1, 0)
+    rows, cosine, sine, own_tags, sent_tags = lax.optimization_barrier(
+        (rows, cosine, sine, own_tags, sent_tags)
+    )
+    sums = partial_sums(rows, (), [], weights, [tokens], True)
+    sums, cosine, sine, own_tags, sent_tags, held[3] = lax.optimization_barrier(
+        (sums, cosine, sine, own_tags, sent_tags, held[3])
+    )
+    receive(2, 1)
+    receive(4, 3)
+    receive(6, 3)
+    receive(5, 4)
+
+    def add(offsets, given):
+        blocks = [held[k] for k in offsets]
+        return partial_sums(rows, offsets, blocks, weights, given, False)
+
+    sums = add((1, 3), sums)
+    sums, held[6] = lax.optimization_barrier((sums, held[6]))
+    receive(7, 6)
+    sums = add((2, 4, 6), sums)
+    query, sent = add((7, 5), sums)
+    got = lax.ppermute(sent, "tp", siblings)
 
     queries, fresh, page = pl.pallas_call(
         rotate_kernel,
@@ -199,23 +208,28 @@
             jax.ShapeDtypeStruct((ROWS, 2 * HD), BF),
             jax.ShapeDtypeStruct((ROWS + 16, HD), BF),
         ],
-        in_specs=[pl.BlockSpec(memory_space=pltpu.SMEM)] + [pl.BlockSpec()] * 6,
+        in_specs=[SMEM] + [VMEM] * 6,
+        out_specs=[VMEM] * 3,
+        compiler_params=pltpu.CompilerParams(vmem_limit_bytes=16 << 20),
         name="rotate",
-    )(core.reshape(1).astype(jnp.int32), query, keyval, got, cosine, sine, sent_tags)
+    )(core.reshape(1).astype(jnp.int32), query, sent, got, cosine, sine, sent_tags)
 
     far = lax.ppermute(page, "row", [(r, (r + 16) % 32) for r in range(32)])
     context = pl.pallas_call(
         attend_kernel,
         out_shape=jax.ShapeDtypeStruct((ROWS, 2 * HD), BF),
-        in_specs=[pl.BlockSpec(memory_space=pltpu.SMEM)] + [pl.BlockSpec()] * 3,
-        compiler_params=pltpu.CompilerParams(vmem_limit_bytes=40 << 20),
+        in_specs=[SMEM] + [VMEM] * 3,
+        out_specs=VMEM,
+        compiler_params=pltpu.CompilerParams(vmem_limit_bytes=32 << 20),
         cost_estimate=pl.CostEstimate(flops=400_000_000, bytes_accessed=1_000_000, transcendentals=700_000),
         name="attend",
     )(prefix_len, queries, fresh, prefix_cache[0])
     packed = pl.pallas_call(
         pack_kernel,
         out_shape=jax.ShapeDtypeStruct((64 * PAGE, HD), BF),
-        compiler_params=pltpu.CompilerParams(vmem_limit_bytes=24 << 20),
+        in_specs=[VMEM] * 3,
+        out_specs=VMEM,
+        compiler_params=pltpu.CompilerParams(vmem_limit_bytes=16 << 20),
         name="pack",
     )(page, own_tags, far)
     received = lax.all_to_all(

time: 100 us -> 85.2 us (0.85)
  waiting for transfers between devices: 31.3 us -> 25.6 us
  local copies, waits for them, and re-layouts: 11.1 us -> 6.35 us
  Pallas kernels: 12.1 us -> 8.3 us
  starting transfers between devices: 36.9 us -> 39.7 us
  blocking collectives: 4.52 us -> 2.21 us
    ppermute x9, waiting for transfers between devices: 15.6 us -> 9.34 us  [the longest x7 7.46 us: receive(): held[got] = lax.ppermute(held[had], 'tp', step_perm(got, had))]
    unnamed x25 -> x9, local copies, waits for them, and re-layouts: 9.05 us -> 4.85 us
    ppermute x1, starting transfers between devices: 6.26 us -> 9.13 us  [shards(): far = lax.ppermute(page, 'row', [(r, (r + 16) % 32) for r in range(32)])]
    all_gather x1, blocking collectives: 4.52 us -> 2.21 us  [shards(): lax.all_gather(tokens, 'tp', axis=0, tiled=True, axis_index_groups=[[2 *...]
    pallas_call x1, Pallas kernels: 2.16 us -> 0.19 us  [shards(): pl.pallas_call(rotate_kernel, out_shape=[jax.ShapeDtypeStruct((2 * ROWS,...]
    pallas_call x2 -> x4, Pallas kernels: 6.26 us -> 4.39 us  [partial_sums(): pl.pallas_call(functools.partial(partial_kernel, offsets, own), out_shape...]
    all_to_all x1, waiting for transfers between devices: 4.19 us -> 6.01 us  [shards(): lax.all_to_all(packed, 'row', 0, 0, tiled=True, axis_index_groups=[[z * 1...]
    ppermute x1, waiting for transfers between devices: 11.5 us -> 10.2 us  [shards(): far = lax.ppermute(page, 'row', [(r, (r + 16) % 32) for r in range(32)])]
  transfers between devices with their start and end apart: 11 -> 11, of which waited for: 5 -> 6; matrix products, arithmetic and copies ran while one was open for 4% -> 3% of each run, Pallas kernels for 6% -> 7%
where the time goes in v2:
time: 85.2 us; the launch traced here: 84.6 us
  starting transfers between devices  39.7 us (47%)
  waiting for transfers between devices  25.6 us (30%)
  Pallas kernels  8.3 us (10%)
  local copies, waits for them, and re-layouts  6.35 us (7%)
  blocking collectives  2.21 us (3%)
  between operations  1.64 us (2%)
  other arithmetic  0.89 us (1%)
    ppermute x7, starting transfers between devices, receive(): held[got] = lax.ppermute(held[had], 'tp', step_perm(got, had))  19.4 us
    ppermute x1, waiting for transfers between devices, shards(): far = lax.ppermute(page, 'row', [(r, (r + 16) % 32) for r in range(32)])  10.2 us
    ppermute x1, starting transfers between devices, shards(): far = lax.ppermute(page, 'row', [(r, (r + 16) % 32) for r in range(32)])  9.13 us
    ppermute x7, waiting for transfers between devices, receive(): held[got] = lax.ppermute(held[had], 'tp', step_perm(got, had))  7.46 us
    all_to_all x1, starting transfers between devices, shards(): lax.all_to_all(packed, 'row', 0, 0, tiled=True, axis_index_groups=[[z * 1...  7.03 us
    all_to_all x1, waiting for transfers between devices, shards(): lax.all_to_all(packed, 'row', 0, 0, tiled=True, axis_index_groups=[[z * 1...  6.01 us
    unnamed x9, local copies, waits for them, and re-layouts  4.85 us
    pallas_call x4, Pallas kernels, partial_sums(): pl.pallas_call(functools.partial(partial_kernel, offsets, own), out_shape...  4.39 us
  transfers between devices with their start and end apart: 11, of which 6 were waited for; matrix products, arithmetic and copies ran while one was open for 3% of the time, Pallas kernels for 7%

profile of v2, /device:TPU:160, one launch (start us, length us, event | category | flops | bytes accessed | tf_op | source)
XLA Modules:
  0.0 84.6 jit_solution(3672117545113918989)
XLA Ops:
  0.6 2.2 %all_gather.3 = bf16[512,256]{1,0:T(8,128)(2,1)S(1)} all-gather(bf16[256,256]{1,0:T(8,128)(2,1)} %refs_3_.2), channel_id=1, replica_groups={{0,1},{2,3},{4,5},{6,7},{8,9},{10,11},{12,13},{14,15},{16,17},{18,19},{..., dimensions={0}, use_global_device_ids=true | all-gather | bytes 393216 | tf_op jit(solution)/shard_map/all_gather | solution.py:142
  2.8 2.0 %collective-permute-start.1 = (bf16[4096,256]{1,0:T(8,128)(2,1)}, bf16[4096,256]{1,0:T(8,128)(2,1)S(1)}, u32[]{:S(2)}, u32[]{:S(2)}) collective-permute-start(bf16[4096,256]{1,0:T(8,128)(2,1)} %refs_2_.5), channel_id=1, source_target_pairs={{0,1},{1,0},{2,3},{3,2},{4,5},{5,4},{6,7},{7,6},{8,9},{9,8},{10,11... | collective-permute-start | bytes 6291464 | tf_op jit(solution)/shard_map/ppermute | solution.py:175
  4.9 1.3 %collective-permute-start.2 = (bf16[512,256]{1,0:T(8,128)(2,1)S(1)}, bf16[512,256]{1,0:T(8,128)(2,1)S(1)}, u32[]{:S(2)}, u32[]{:S(2)}) collective-permute-start(bf16[512,256]{1,0:T(8,128)(2,1)S(1)} %all_gather.3), channel_id=1, source_target_pairs={{0,6},{2,8},{4,10},{6,12},{8,14},{7,1},{9,3},{11,5},{13,7},{15,9},... | collective-permute-start | bytes 786440 | tf_op jit(solution)/shard_map/ppermute | solution.py:172
  6.2 3.8 %collective-permute-start = (bf16[512,256]{1,0:T(8,128)(2,1)S(1)}, bf16[512,256]{1,0:T(8,128)(2,1)S(1)}, u32[]{:S(2)}, u32[]{:S(2)}) collective-permute-start(bf16[512,256]{1,0:T(8,128)(2,1)S(1)} %all_gather.3), channel_id=1, source_target_pairs={{0,2},{2,4},{4,6},{6,8},{8,10},{10,12},{12,14},{3,1},{5,3},{7,5},{... | collective-permute-start | bytes 786440 | tf_op jit(solution)/shard_map/ppermute | solution.py:172
  10.0 0.8 copy.24
  10.8 0.1 eq.45
  10.9 0.2 convert_reduce_fusion
  11.1 0.1 reduce_sum.12
  11.9 0.5 fusion
  12.4 0.1 pad_maximum_fusion
  12.6 0.1 copy.29
  12.7 0.1 broadcast_in_dim.16
  12.8 0.1 reshape_reshape.8
  12.8 0.1 copy.30
  12.9 0.1 broadcast_in_dim.17
  13.0 0.1 reshape_reshape.9
  13.2 0.1 stack.35.rows_ref
  13.3 0.0 collective-permute-done.1.refs_1_.refs_3_.refs_4_
  13.3 0.0 copy-start
  13.3 1.6 %copy-done = bf16[4096,256]{1,0:T(8,128)(2,1)S(1)} copy-done((bf16[4096,256]{1,0:T(8,128)(2,1)S(1)}, bf16[4096,256]{1,0:T(8,128)(2,1)}, u32[]{:S(2)}) %copy-start) | copy-done | bytes 2097176
  14.9 1.6 %copy-done.1 = bf16[4096,256]{1,0:T(8,128)(2,1)S(1)} copy-done((bf16[4096,256]{1,0:T(8,128)(2,1)S(1)}, bf16[4096,256]{1,0:T(8,128)(2,1)}, u32[]{:S(2)}) %copy-start.1) | copy-done | bytes 2097176
  16.5 0.9 %copy-done.2 = bf16[256,256]{1,0:T(8,128)(2,1)S(1)} copy-done((bf16[256,256]{1,0:T(8,128)(2,1)S(1)}, bf16[256,256]{1,0:T(8,128)(2,1)}, u32[]{:S(2)}) %copy-start.2) | copy-done | bytes 131096
  17.4 0.8 partial_sums.4
  18.2 1.8 %collective-permute-done.2.refs_1_ = bf16[512,256]{1,0:T(8,128)(2,1)S(1)} collective-permute-done((bf16[512,256]{1,0:T(8,128)(2,1)S(1)}, bf16[512,256]{1,0:T(8,128)(2,1)S(1)}, u32[]{:S(2)}, u32[]{:S(2)}) %collective-permute-start.2) | collective-permute-done | bytes 262176 | tf_op jit(solution)/shard_map/ppermute | solution.py:172
  20.0 0.7 collective-permute-start.3
  20.7 6.2 %collective-permute-start.5 = (bf16[512,256]{1,0:T(8,128)(2,1)S(1)}, bf16[512,256]{1,0:T(8,128)(2,1)S(1)}, u32[]{:S(2)}, u32[]{:S(2)}) collective-permute-start(bf16[512,256]{1,0:T(8,128)(2,1)S(1)} %collective-permute-done.2.refs_1_), channel_id=1, source_target_pairs={{6,8},{8,10},{10,12},{12,14},{3,1},{5,3},{7,5},{9,7},{22,24},{24,2... | collective-permute-start | bytes 786440 | tf_op jit(solution)/shard_map/ppermute | solution.py:172
  26.9 0.0 collective-permute-done.refs_0_
  26.9 1.9 %collective-permute-start.7 = (bf16[512,256]{1,0:T(8,128)(2,1)S(1)}, bf16[512,256]{1,0:T(8,128)(2,1)S(1)}, u32[]{:S(2)}, u32[]{:S(2)}) collective-permute-start(bf16[512,256]{1,0:T(8,128)(2,1)S(1)} %collective-permute-done.refs_0_), channel_id=1, source_target_pairs={{2,4},{4,6},{6,8},{8,10},{10,12},{12,14},{3,1},{5,3},{7,5},{9,7},{... | collective-permute-start | bytes 786440 | tf_op jit(solution)/shard_map/ppermute | solution.py:172
  28.8 1.1 %partial_sums.5 = (f32[256,256]{1,0:T(8,128)S(1)}, f32[256,512]{1,0:T(8,128)S(1)}) custom-call(s32[8]{0:T(128)S(1)} %stack.35.rows_ref, bf16[512,256]{1,0:T(8,128)(2,1)S(1)} %collective-permute-done.refs_0_, bf16[512,256]{1,0:T(8,128)(2,1)S(1)} %collective-permute-done.2.refs_1_, bf16[4096,256]{1,0:T(8,128)(2,1)S(1)} %copy-done, ...), custom_call_target="tpu_custom_call" | custom-call | flops 402653184 | bytes 2097152 | tf_op jit(solution)/shard_map/partial_sums/pallas_call | solution.py:54
  30.0 0.0 collective-permute-done.3.refs_2_
  30.0 0.7 collective-permute-start.4
  30.7 2.9 %collective-permute-done.5.refs_1_ = bf16[512,256]{1,0:T(8,128)(2,1)S(1)} collective-permute-done((bf16[512,256]{1,0:T(8,128)(2,1)S(1)}, bf16[512,256]{1,0:T(8,128)(2,1)S(1)}, u32[]{:S(2)}, u32[]{:S(2)}) %collective-permute-start.5) | collective-permute-done | bytes 262176 | tf_op jit(solution)/shard_map/ppermute | solution.py:172
  33.6 4.8 %collective-permute-start.6 = (bf16[512,256]{1,0:T(8,128)(2,1)S(1)}, bf16[512,256]{1,0:T(8,128)(2,1)S(1)}, u32[]{:S(2)}, u32[]{:S(2)}) collective-permute-start(bf16[512,256]{1,0:T(8,128)(2,1)S(1)} %collective-permute-done.5.refs_1_), channel_id=1, source_target_pairs={{8,10},{10,12},{12,14},{3,1},{5,3},{7,5},{24,26},{26,28},{28,30},{... | collective-permute-start | bytes 786440 | tf_op jit(solution)/shard_map/ppermute | solution.py:172
  38.4 0.0 collective-permute-done.7.refs_0_
  38.4 1.3 %partial_sums.6 = (f32[256,256]{1,0:T(8,128)S(1)}, f32[256,512]{1,0:T(8,128)S(1)}) custom-call(s32[8]{0:T(128)S(1)} %stack.35.rows_ref, bf16[512,256]{1,0:T(8,128)(2,1)S(1)} %collective-permute-done.7.refs_0_, bf16[512,256]{1,0:T(8,128)(2,1)S(1)} %collective-permute-done.5.refs_1_, bf16[512,256]{1,0:T(8,128)(2,1)S(1)} %collective-permute-done.3.refs_2_, ...), custom_call_target="tpu_custom_call" | custom-call | flops 603979776 | bytes 3145728 | tf_op jit(solution)/shard_map/partial_sums/pallas_call | solution.py:54
  39.7 2.7 %collective-permute-done.6.refs_1_ = bf16[512,256]{1,0:T(8,128)(2,1)S(1)} collective-permute-done((bf16[512,256]{1,0:T(8,128)(2,1)S(1)}, bf16[512,256]{1,0:T(8,128)(2,1)S(1)}, u32[]{:S(2)}, u32[]{:S(2)}) %collective-permute-start.6) | collective-permute-done | bytes 262176 | tf_op jit(solution)/shard_map/ppermute | solution.py:172
  42.5 1.1 %partial_sums.7 = (f32[256,256]{1,0:T(8,128)S(1)}, f32[256,512]{1,0:T(8,128)S(1)}) custom-call(s32[8]{0:T(128)S(1)} %stack.35.rows_ref, bf16[512,256]{1,0:T(8,128)(2,1)S(1)} %collective-permute-done.4.refs_0_, bf16[512,256]{1,0:T(8,128)(2,1)S(1)} %collective-permute-done.6.refs_1_, bf16[4096,256]{1,0:T(8,128)(2,1)S(1)} %copy-done, ...), custom_call_target="tpu_custom_call" | custom-call | flops 402653184 | bytes 2097152 | tf_op jit(solution)/shard_map/partial_sums/pallas_call | solution.py:54
  43.6 0.0 copy-start.3
  43.6 2.1 %collective-permute-start.8 = (f32[256,512]{1,0:T(8,128)S(1)}, f32[256,512]{1,0:T(8,128)S(1)}, u32[]{:S(2)}, u32[]{:S(2)}) collective-permute-start(f32[256,512]{1,0:T(8,128)S(1)} %get-tuple-element.48.sent_ref), channel_id=1, source_target_pairs={{0,1},{1,0},{2,3},{3,2},{4,5},{5,4},{6,7},{7,6},{8,9},{9,8},{10,11... | collective-permute-start | bytes 1572872 | tf_op jit(solution)/shard_map/ppermute | solution.py:202
  45.7 1.9 %collective-permute-done.8.got_ref = f32[256,512]{1,0:T(8,128)S(1)} collective-permute-done((f32[256,512]{1,0:T(8,128)S(1)}, f32[256,512]{1,0:T(8,128)S(1)}, u32[]{:S(2)}, u32[]{:S(2)}) %collective-permute-start.8) | collective-permute-done | bytes 524320 | tf_op jit(solution)/shard_map/ppermute | solution.py:202
  47.5 0.2 rotate.1
  47.7 9.1 %collective-permute-start.9 = (bf16[272,128]{1,0:T(8,128)(2,1)S(1)}, bf16[272,128]{1,0:T(8,128)(2,1)S(1)}, u32[]{:S(2)}, u32[]{:S(2)}) collective-permute-start(bf16[272,128]{1,0:T(8,128)(2,1)S(1)} %get-tuple-element.54.own_ref), channel_id=1, source_target_pairs={{0,256},{16,272},{32,288},{48,304},{64,320},{80,336},{96,352},{112... | collective-permute-start | bytes 208904 | tf_op jit(solution)/shard_map/ppermute | solution.py:217
  56.9 10.2 %collective-permute-done.9.got_ref = bf16[272,128]{1,0:T(8,128)(2,1)S(1)} collective-permute-done((bf16[272,128]{1,0:T(8,128)(2,1)S(1)}, bf16[272,128]{1,0:T(8,128)(2,1)S(1)}, u32[]{:S(2)}, u32[]{:S(2)}) %collective-permute-start.9) | collective-permute-done | bytes 69664 | tf_op jit(solution)/shard_map/ppermute | solution.py:217
  67.1 1.3 %pack.1 = bf16[1024,128]{1,0:T(8,128)(2,1)} custom-call(bf16[272,128]{1,0:T(8,128)(2,1)S(1)} %get-tuple-element.54.own_ref, bf16[16,128]{1,0:T(8,128)(2,1)S(1)} %concatenate.14.tag_ref, bf16[272,128]{1,0:T(8,128)(2,1)S(1)} %collective-permute-done.9.got_ref), custom_call_target="tpu_custom_call" | custom-call | tf_op jit(solution)/shard_map/pack/pallas_call | solution.py:227
  68.4 7.0 %all-to-all-start = ((bf16[16,64,128]{2,1,0:T(8,128)(2,1)}), bf16[16,64,128]{2,1,0:T(8,128)(2,1)S(1)}, u32[]{:S(2)}, u32[]{:S(2)}) async-start(bf16[16,64,128]{2,1,0:T(8,128)(2,1)} %bitcast.13), calls=%async_computation | async-start | bytes 524288 | tf_op jit(solution)/shard_map/all_to_all | solution.py:235
  75.5 2.4 %attend.1 = bf16[256,256]{1,0:T(8,128)(2,1)} custom-call(s32[1]{0:T(128)S(6)} %copy.32.len_ref, bf16[512,128]{1,0:T(8,128)(2,1)S(1)} %get-tuple-element.52.query_ref, bf16[256,256]{1,0:T(8,128)(2,1)S(1)} %get-tuple-element.53.fresh_ref, bf16[1024,256]{1,0:T(8,128)(2,1)S(1)} %bitcast.20), custom_call_target="tpu_custom_call" | custom-call | flops 400000000 | bytes 1000000 | tf_op jit(solution)/shard_map/attend/pallas_call | solution.py:218
  77.9 6.0 %all-to-all-done = bf16[16,64,128]{2,1,0:T(8,128)(2,1)S(1)} async-done(((bf16[16,64,128]{2,1,0:T(8,128)(2,1)}), bf16[16,64,128]{2,1,0:T(8,128)(2,1)S(1)}, u32[]{:S(2)}, u32[]{:S(2)}) %all-to-all-start) | async-done | bytes 262176 | tf_op jit(solution)/shard_map/all_to_all | solution.py:235
  83.9 0.7 copy.31
  (9 shorter events, 0.1 us)
Async XLA Ops:
  2.8 10.4 %collective-permute-start.1 = (bf16[4096,256]{1,0:T(8,128)(2,1)}, bf16[4096,256]{1,0:T(8,128)(2,1)S(1)}, u32[]{:S(2)}, u32[]{:S(2)}) collective-permute-start(bf16[4096,256]{1,0:T(8,128)(2,1)} %refs_2_.5), channel_id=1, source_target_pairs={{0,1},{1,0},{2,3},{3,2},{4,5},{5,4},{6,7},{7,6},{8,9},{9,8},{10,11... | collective-permute-start | bytes 6291464 | tf_op jit(solution)/shard_map/ppermute | solution.py:175
  4.9 15.1 %collective-permute-start.2 = (bf16[512,256]{1,0:T(8,128)(2,1)S(1)}, bf16[512,256]{1,0:T(8,128)(2,1)S(1)}, u32[]{:S(2)}, u32[]{:S(2)}) collective-permute-start(bf16[512,256]{1,0:T(8,128)(2,1)S(1)} %all_gather.3), channel_id=1, source_target_pairs={{0,6},{2,8},{4,10},{6,12},{8,14},{7,1},{9,3},{11,5},{13,7},{15,9},... | collective-permute-start | bytes 786440 | tf_op jit(solution)/shard_map/ppermute | solution.py:172
  6.2 20.7 %collective-permute-start = (bf16[512,256]{1,0:T(8,128)(2,1)S(1)}, bf16[512,256]{1,0:T(8,128)(2,1)S(1)}, u32[]{:S(2)}, u32[]{:S(2)}) collective-permute-start(bf16[512,256]{1,0:T(8,128)(2,1)S(1)} %all_gather.3), channel_id=1, source_target_pairs={{0,2},{2,4},{4,6},{6,8},{8,10},{10,12},{12,14},{3,1},{5,3},{7,5},{... | collective-permute-start | bytes 786440 | tf_op jit(solution)/shard_map/ppermute | solution.py:172
  13.3 1.6 %copy-start = (bf16[4096,256]{1,0:T(8,128)(2,1)S(1)}, bf16[4096,256]{1,0:T(8,128)(2,1)}, u32[]{:S(2)}) copy-start(bf16[4096,256]{1,0:T(8,128)(2,1)} %refs_2_.5) | copy-start | bytes 6291460
  14.9 1.6 %copy-start.1 = (bf16[4096,256]{1,0:T(8,128)(2,1)S(1)}, bf16[4096,256]{1,0:T(8,128)(2,1)}, u32[]{:S(2)}) copy-start(bf16[4096,256]{1,0:T(8,128)(2,1)} %refs_4_.3) | copy-start | bytes 6291460
  16.5 0.9 %copy-start.2 = (bf16[256,256]{1,0:T(8,128)(2,1)S(1)}, bf16[256,256]{1,0:T(8,128)(2,1)}, u32[]{:S(2)}) copy-start(bf16[256,256]{1,0:T(8,128)(2,1)} %refs_3_.2) | copy-start | bytes 393220
  20.0 10.0 %collective-permute-start.3 = (bf16[512,256]{1,0:T(8,128)(2,1)S(1)}, bf16[512,256]{1,0:T(8,128)(2,1)S(1)}, u32[]{:S(2)}, u32[]{:S(2)}) collective-permute-start(bf16[512,256]{1,0:T(8,128)(2,1)S(1)} %collective-permute-done.2.refs_1_), channel_id=1, source_target_pairs={{6,12},{8,14},{7,1},{9,3},{22,28},{24,30},{23,17},{25,19},{38,44},... | collective-permute-start | bytes 786440 | tf_op jit(solution)/shard_map/ppermute | solution.py:172
  20.7 12.9 %collective-permute-start.5 = (bf16[512,256]{1,0:T(8,128)(2,1)S(1)}, bf16[512,256]{1,0:T(8,128)(2,1)S(1)}, u32[]{:S(2)}, u32[]{:S(2)}) collective-permute-start(bf16[512,256]{1,0:T(8,128)(2,1)S(1)} %collective-permute-done.2.refs_1_), channel_id=1, source_target_pairs={{6,8},{8,10},{10,12},{12,14},{3,1},{5,3},{7,5},{9,7},{22,24},{24,2... | collective-permute-start | bytes 786440 | tf_op jit(solution)/shard_map/ppermute | solution.py:172
  26.9 11.5 %collective-permute-start.7 = (bf16[512,256]{1,0:T(8,128)(2,1)S(1)}, bf16[512,256]{1,0:T(8,128)(2,1)S(1)}, u32[]{:S(2)}, u32[]{:S(2)}) collective-permute-start(bf16[512,256]{1,0:T(8,128)(2,1)S(1)} %collective-permute-done.refs_0_), channel_id=1, source_target_pairs={{2,4},{4,6},{6,8},{8,10},{10,12},{12,14},{3,1},{5,3},{7,5},{9,7},{... | collective-permute-start | bytes 786440 | tf_op jit(solution)/shard_map/ppermute | solution.py:172
  30.0 9.8 %collective-permute-start.4 = (bf16[512,256]{1,0:T(8,128)(2,1)S(1)}, bf16[512,256]{1,0:T(8,128)(2,1)S(1)}, u32[]{:S(2)}, u32[]{:S(2)}) collective-permute-start(bf16[512,256]{1,0:T(8,128)(2,1)S(1)} %collective-permute-done.3.refs_2_), channel_id=1, source_target_pairs={{12,14},{3,1},{28,30},{19,17},{44,46},{35,33},{60,62},{51,49},{76,... | collective-permute-start | bytes 786440 | tf_op jit(solution)/shard_map/ppermute | solution.py:172
  33.6 8.9 %collective-permute-start.6 = (bf16[512,256]{1,0:T(8,128)(2,1)S(1)}, bf16[512,256]{1,0:T(8,128)(2,1)S(1)}, u32[]{:S(2)}, u32[]{:S(2)}) collective-permute-start(bf16[512,256]{1,0:T(8,128)(2,1)S(1)} %collective-permute-done.5.refs_1_), channel_id=1, source_target_pairs={{8,10},{10,12},{12,14},{3,1},{5,3},{7,5},{24,26},{26,28},{28,30},{... | collective-permute-start | bytes 786440 | tf_op jit(solution)/shard_map/ppermute | solution.py:172
  43.6 31.9 %copy-start.3 = (bf16[1,1024,256]{2,1,0:T(8,128)(2,1)S(1)}, bf16[1,1024,256]{2,1,0:T(8,128)(2,1)}, u32[]{:S(2)}) copy-start(bf16[1,1024,256]{2,1,0:T(8,128)(2,1)} %param.9) | copy-start | bytes 1572868
  43.6 3.9 %collective-permute-start.8 = (f32[256,512]{1,0:T(8,128)S(1)}, f32[256,512]{1,0:T(8,128)S(1)}, u32[]{:S(2)}, u32[]{:S(2)}) collective-permute-start(f32[256,512]{1,0:T(8,128)S(1)} %get-tuple-element.48.sent_ref), channel_id=1, source_target_pairs={{0,1},{1,0},{2,3},{3,2},{4,5},{5,4},{6,7},{7,6},{8,9},{9,8},{10,11... | collective-permute-start | bytes 1572872 | tf_op jit(solution)/shard_map/ppermute | solution.py:202
  47.7 19.4 %collective-permute-start.9 = (bf16[272,128]{1,0:T(8,128)(2,1)S(1)}, bf16[272,128]{1,0:T(8,128)(2,1)S(1)}, u32[]{:S(2)}, u32[]{:S(2)}) collective-permute-start(bf16[272,128]{1,0:T(8,128)(2,1)S(1)} %get-tuple-element.54.own_ref), channel_id=1, source_target_pairs={{0,256},{16,272},{32,288},{48,304},{64,320},{80,336},{96,352},{112... | collective-permute-start | bytes 208904 | tf_op jit(solution)/shard_map/ppermute | solution.py:217
  68.4 15.5 %all-to-all-start = ((bf16[16,64,128]{2,1,0:T(8,128)(2,1)}), bf16[16,64,128]{2,1,0:T(8,128)(2,1)S(1)}, u32[]{:S(2)}, u32[]{:S(2)}) async-start(bf16[16,64,128]{2,1,0:T(8,128)(2,1)} %bitcast.13), calls=%async_computation | async-start | bytes 524288 | tf_op jit(solution)/shard_map/all_to_all | solution.py:235
